TPU v7x, 32 devices: a whole 2x2x4 slice. The times are simulated.
32 devices in a mesh: blk: 16 (over z, y, core), dp: 2 (over x).
Axes of the slice: x: 2, y: 2, z: 4, core: 2. Of those that a mesh axis runs over, the one named last changes fastest.
Arguments:
- acts: bfloat16 [2, 4608, 2048], P(None, ('blk', 'dp')), may hold values from -6 to 6
- cotangent: bfloat16 [2, 4608, 2048], P(None, ('blk', 'dp')), may hold values from -6 to 6
- w_gate: bfloat16 [16, 2048, 128], P('blk', 'dp'), may hold values from -0.125 to 0.125
- w_up: bfloat16 [16, 2048, 128], P('blk', 'dp'), may hold values from -0.125 to 0.125
- w_down: bfloat16 [16, 128, 2048], P('blk', None, 'dp'), may hold values from -0.078125 to 0.078125
- slab_layer: int32 [16], replicated, may hold values from 0 to 1
Outputs:
- grad_gate: bfloat16 [16, 2048, 128], P('blk', 'dp')
- grad_up: bfloat16 [16, 2048, 128], P('blk', 'dp')
- grad_down: bfloat16 [16, 128, 2048], P('blk', None, 'dp')
- acts_grad: bfloat16 [2, 4608, 2048], P(None, ('blk', 'dp'))
All inputs are finite; a program needn't handle non-finite values.
Results may differ from a plain program's by a relative error of at most 0.0049.
Values may be sent and summed in bfloat16 or wider, within the bound.
A program may use at most 64 MiB of HBM per device.

v0:
```python
import jax
import jax.numpy as jnp
from jax import lax
from jax.sharding import PartitionSpec as P

TICKS = 3


def shifted(block, axis, distance):
    devices = range(lax.axis_size(axis))
    route = [((i - distance) % len(devices), i) for i in devices]
    return lax.ppermute(block, axis, route)


def slab_terms(rows_x, rows_g, w_gate, w_up, w_down):
    gate = jnp.dot(rows_x, w_gate, preferred_element_type=jnp.float32)
    upward = jnp.dot(rows_x, w_up, preferred_element_type=jnp.float32)
    sigmoid_gate = jax.nn.sigmoid(gate)
    activated = gate * sigmoid_gate
    hidden = (activated * upward).astype(jnp.bfloat16)
    by_units = (((1,), (1,)), ((), ()))
    by_rows = (((0,), (0,)), ((), ()))
    hidden_grad = lax.dot_general(rows_g, w_down, by_units, preferred_element_type=jnp.float32)
    up_in = (hidden_grad * activated).astype(jnp.bfloat16)
    gate_in = (hidden_grad * upward * sigmoid_gate * (1.0 + gate * (1.0 - sigmoid_gate))).astype(
        jnp.bfloat16
    )
    grad_gate = lax.dot_general(rows_x, gate_in, by_rows, preferred_element_type=jnp.float32)
    grad_upw = lax.dot_general(rows_x, up_in, by_rows, preferred_element_type=jnp.float32)
    grad_down = lax.dot_general(hidden, rows_g, by_rows, preferred_element_type=jnp.float32)
    input_grad = lax.dot_general(gate_in, w_gate, by_units, preferred_element_type=jnp.float32)
    input_grad = input_grad + lax.dot_general(
        up_in, w_up, by_units, preferred_element_type=jnp.float32
    )
    return ((grad_gate, grad_upw, grad_down), input_grad)


def layer_rows(stack, layer):
    return lax.dynamic_index_in_dim(stack, layer, 0, keepdims=False)


def add_layer(total, layer, piece):
    current = lax.dynamic_index_in_dim(total, layer, 0, keepdims=False)
    return lax.dynamic_update_index_in_dim(total, current + piece, layer, 0)


def add_terms(first, second):
    return (first[0] + second[0], first[1] + second[1], first[2] + second[2])


def on_device(acts, cotangent, w_gate, w_up, w_down, slab_layer):
    whole = (
        lax.all_gather(w_gate, "dp", axis=1, tiled=True),
        lax.all_gather(w_up, "dp", axis=1, tiled=True),
        lax.all_gather(w_down, "dp", axis=2, tiled=True),
    )
    own_slab = (whole[0][0], whole[1][0], whole[2][0])
    cycle_size = lax.axis_size("blk")
    position = lax.axis_index("blk")
    input_total = jnp.zeros(acts.shape, jnp.float32)
    sums = None
    for tick in range(TICKS):
        layer = slab_layer[(position - tick) % cycle_size]
        if tick == 0:
            rows_x = layer_rows(acts, layer)
            rows_g = layer_rows(cotangent, layer)
        else:
            rows_x, rows_g = shifted(
                (layer_rows(acts, layer), layer_rows(cotangent, layer)), "blk", -tick
            )
        terms, input_grad = slab_terms(rows_x, rows_g, own_slab[0], own_slab[1], own_slab[2])
        sums = terms if tick == 0 else add_terms(sums, terms)
        if tick == 0:
            input_total = add_layer(input_total, layer, input_grad)
        else:
            returned = shifted(input_grad, "blk", tick)
            input_total = add_layer(input_total, layer, returned)
    halves = (
        lax.psum_scatter(sums[0], "dp", scatter_dimension=0, tiled=True),
        lax.psum_scatter(sums[1], "dp", scatter_dimension=0, tiled=True),
        lax.psum_scatter(sums[2], "dp", scatter_dimension=1, tiled=True),
    )
    return (
        halves[0].astype(jnp.bfloat16)[None],
        halves[1].astype(jnp.bfloat16)[None],
        halves[2].astype(jnp.bfloat16)[None],
        input_total.astype(jnp.bfloat16),
    )


def solution(mesh):
    in_specs = (
        P(None, ("blk", "dp"), None),
        P(None, ("blk", "dp"), None),
        P("blk", "dp", None),
        P("blk", "dp", None),
        P("blk", None, "dp"),
        P(),
    )
    out_specs = (
        P("blk", "dp", None),
        P("blk", "dp", None),
        P("blk", None, "dp"),
        P(None, ("blk", "dp"), None),
    )
    return jax.shard_map(
        on_device, mesh=mesh, in_specs=in_specs, out_specs=out_specs, check_vma=False
    )
```

profile of v0, /device:TPU:0, one launch (start us, length us, event | category | flops | bytes accessed | tf_op | source)
XLA Modules:
  0.0 139.8 jit_solution(14244294822490813206)
XLA Ops:
  7.3 1.4 fusion.59
  12.5 2.5 %dynamic-slice_bitcast_fusion.1 = (bf16[144,2048]{1,0:T(8,128)(2,1)}, bf16[144,2048]{1,0:T(8,128)(2,1)}) fusion(bf16[2,144,2048]{2,1,0:T(8,128)(2,1)} %param.6, s32[]{:T(128)S(6)} %select_n.53, s32[]{:T(128)S(6)} %select_n.50), kind=kLoop, calls=%fused_computation.28 | loop fusion | bytes 2359304 | tf_op jit(solution)/shard_map/jit(dynamic_index_in_dim)/squeeze | solution.py:39
  15.0 5.4 %collective-permute-start = (bf16[144,2048]{1,0:T(8,128)(2,1)}, bf16[144,2048]{1,0:T(8,128)(2,1)S(1)}, u32[]{:S(2)}, u32[]{:S(2)}) collective-permute-start(bf16[144,2048]{1,0:T(8,128)(2,1)} %get-tuple-element.7), channel_id=1, source_target_pairs={{2,0},{4,2},{6,4},{8,6},{10,8},{12,10},{14,12},{16,14},{18,16},{20... | collective-permute-start | bytes 1769480 | tf_op jit(solution)/shard_map/ppermute | solution.py:12
  20.5 1.1 dynamic-slice_bitcast_fusion
  21.6 0.7 collective-permute-start.1
  22.8 1.4 %collective-permute-start.3 = (bf16[144,2048]{1,0:T(8,128)(2,1)}, bf16[144,2048]{1,0:T(8,128)(2,1)}, u32[]{:S(2)}, u32[]{:S(2)}) collective-permute-start(bf16[144,2048]{1,0:T(8,128)(2,1)} %get-tuple-element.4), channel_id=1, source_target_pairs={{4,0},{6,2},{8,4},{10,6},{12,8},{14,10},{16,12},{18,14},{20,16},{2... | collective-permute-start | bytes 1769480 | tf_op jit(solution)/shard_map/ppermute | solution.py:12
  25.5 8.2 %all_gather.11 = bf16[1,2048,128]{2,1,0:T(8,128)(2,1)S(1)} all-gather(bf16[1,1024,128]{2,1,0:T(8,128)(2,1)S(1)} %copy-done.12), channel_id=1, replica_groups=mesh['blk'=16,'dp'=2] {'dp'}, dimensions={1}, use_global_device_ids=true | all-gather | bytes 786432 | tf_op jit(solution)/shard_map/all_gather | solution.py:53
  33.6 7.4 %all_gather.10 = bf16[1,2048,128]{2,1,0:T(8,128)(2,1)S(1)} all-gather(bf16[1,1024,128]{2,1,0:T(8,128)(2,1)} %param.9), channel_id=1, replica_groups=mesh['blk'=16,'dp'=2] {'dp'}, dimensions={1}, use_global_device_ids=true | all-gather | bytes 786432 | tf_op jit(solution)/shard_map/all_gather | solution.py:54
  42.7 7.0 %all_gather.9 = bf16[1,128,2048]{2,1,0:T(8,128)(2,1)S(1)} all-gather(bf16[1,128,1024]{2,1,0:T(8,128)(2,1)S(1)} %copy-done.13), channel_id=1, replica_groups=mesh['blk'=16,'dp'=2] {'dp'}, dimensions={2}, use_global_device_ids=true | all-gather | bytes 786432 | tf_op jit(solution)/shard_map/all_gather | solution.py:55
  49.7 0.9 multiply_convert_fusion.5
  51.8 1.6 %collective-permute-done.2 = bf16[144,2048]{1,0:T(8,128)(2,1)S(1)} collective-permute-done((bf16[144,2048]{1,0:T(8,128)(2,1)}, bf16[144,2048]{1,0:T(8,128)(2,1)S(1)}, u32[]{:S(2)}, u32[]{:S(2)}) %collective-permute-start.2) | collective-permute-done | bytes 589856 | tf_op jit(solution)/shard_map/ppermute | solution.py:12
  54.1 2.0 %multiply_convert_fusion.4 = (bf16[144,128]{1,0:T(8,128)(2,1)}, bf16[144,128]{1,0:T(8,128)(2,1)S(1)}) fusion(f32[144,128]{1,0:T(8,128)S(1)} %fusion.22, f32[144,128]{1,0:T(8,128)S(1)} %fusion.30, bf16[144,2048]{1,0:T(8,128)(2,1)} %collective-permute-done.1, bf16[1,128,2048]{2,1,0:T(8,128)(2,1)S(1)} %all_gather.9), kind=kOutput, calls=%fused_computation.68 | convolution fusion | flops 75737088 | bytes 1335296 | tf_op jit(solution)/shard_map/dot_general | solution.py:23
  56.2 0.5 convolution_add_fusion.8
  56.8 3.0 %collective-permute-done.3 = bf16[144,2048]{1,0:T(8,128)(2,1)} collective-permute-done((bf16[144,2048]{1,0:T(8,128)(2,1)}, bf16[144,2048]{1,0:T(8,128)(2,1)}, u32[]{:S(2)}, u32[]{:S(2)}) %collective-permute-start.3) | collective-permute-done | bytes 589856 | tf_op jit(solution)/shard_map/ppermute | solution.py:12
  59.8 2.0 %multiply_convert_fusion.3 = (bf16[144,128]{1,0:T(8,128)(2,1)}, bf16[144,128]{1,0:T(8,128)(2,1)S(1)}) fusion(f32[144,128]{1,0:T(8,128)S(1)} %fusion.20, f32[144,128]{1,0:T(8,128)S(1)} %fusion.28, bf16[144,2048]{1,0:T(8,128)(2,1)} %collective-permute-done.3, bf16[1,128,2048]{2,1,0:T(8,128)(2,1)S(1)} %all_gather.9), kind=kOutput, calls=%fused_computation.67 | convolution fusion | flops 75737088 | bytes 1335296 | tf_op jit(solution)/shard_map/dot_general | solution.py:23
  61.8 0.6 copy-done.16
  62.4 1.5 %convolution_add_fusion.7 = f32[2048,128]{1,0:T(8,128)} fusion(f32[2048,128]{1,0:T(8,128)S(1)} %convolution_add_fusion.8, bf16[144,2048]{1,0:T(8,128)(2,1)S(1)} %collective-permute-done.2, bf16[144,128]{1,0:T(8,128)(2,1)S(1)} %get-tuple-element.9), kind=kOutput, calls=%fused_computation.9 | convolution fusion | flops 75759616 | bytes 2723840 | tf_op jit(solution)/shard_map/dot_general | solution.py:28
  64.0 1.3 fusion.6
  66.1 1.5 %convolution_add_fusion.5 = f32[2048,128]{1,0:T(8,128)} fusion(f32[2048,128]{1,0:T(8,128)S(1)} %convolution_add_fusion.6, bf16[144,2048]{1,0:T(8,128)(2,1)S(1)} %collective-permute-done.2, bf16[144,128]{1,0:T(8,128)(2,1)S(1)} %copy-done.20), kind=kOutput, calls=%fused_computation.7 | convolution fusion | flops 75759616 | bytes 2723840 | tf_op jit(solution)/shard_map/dot_general | solution.py:29
  68.0 1.1 fusion.18
  71.0 1.3 convolution_add_fusion
  72.7 1.4 %convolution_add_fusion.4 = f32[128,2048]{1,0:T(8,128)S(1)} fusion(f32[128,2048]{1,0:T(8,128)S(1)} %fusion.2, bf16[144,2048]{1,0:T(8,128)(2,1)} %collective-permute-done.1, f32[144,128]{1,0:T(8,128)S(1)} %fusion.30, f32[144,128]{1,0:T(8,128)S(1)} %fusion.22), kind=kOutput, calls=%fused_computation.6 | convolution fusion | flops 75870208 | bytes 2834432 | tf_op jit(solution)/shard_map/dot_general | solution.py:30
  74.1 2.4 %convolution_add_fusion.3 = f32[128,2048]{1,0:T(8,128)} fusion(f32[128,2048]{1,0:T(8,128)S(1)} %convolution_add_fusion.4, bf16[144,2048]{1,0:T(8,128)(2,1)} %collective-permute-done.3, f32[144,128]{1,0:T(8,128)S(1)} %copy-done.7, f32[144,128]{1,0:T(8,128)S(1)} %copy-done.5), kind=kOutput, calls=%fused_computation.5 | convolution fusion | flops 75870208 | bytes 2834432 | tf_op jit(solution)/shard_map/dot_general | solution.py:30
  77.7 20.2 %collective-permute-done.4 = f32[144,2048]{1,0:T(8,128)} collective-permute-done((f32[144,2048]{1,0:T(8,128)S(1)}, f32[144,2048]{1,0:T(8,128)}, u32[]{:S(2)}, u32[]{:S(2)}) %collective-permute-start.4) | collective-permute-done | bytes 1179680 | tf_op jit(solution)/shard_map/ppermute | solution.py:12
  98.0 1.5 %bitcast_dynamic-update-slice_fusion.1 = f32[2,144,2048]{2,1,0:T(8,128)S(1)} fusion(f32[2,144,2048]{2,1,0:T(8,128)S(1)} %fusion.1, s32[]{:T(128)S(6)} %select_n.50, f32[144,2048]{1,0:T(8,128)} %collective-permute-done.4, f32[1,144,2048]{2,1,0:T(8,128)S(1)} %constant_dynamic-slice_fusion.1), kind=kLoop, calls=%fused_computation.13 | loop fusion | flops 294912 | bytes 3538948 | tf_op jit(solution)/shard_map/jit(dynamic_update_index_in_dim)/dynamic_update_slice | solution.py:44
  99.5 5.1 %collective-permute-done.5 = f32[144,2048]{1,0:T(8,128)} collective-permute-done((f32[144,2048]{1,0:T(8,128)}, f32[144,2048]{1,0:T(8,128)}, u32[]{:S(2)}, u32[]{:S(2)}) %collective-permute-start.5) | collective-permute-done | bytes 1179680 | tf_op jit(solution)/shard_map/ppermute | solution.py:12
  104.7 1.5 %bitcast_dynamic-update-slice_fusion = f32[2,144,2048]{2,1,0:T(8,128)S(1)} fusion(f32[2,144,2048]{2,1,0:T(8,128)S(1)} %bitcast_dynamic-update-slice_fusion.1, s32[]{:T(128)S(6)} %select_n.53, f32[144,2048]{1,0:T(8,128)} %collective-permute-done.5, f32[1,144,2048]{2,1,0:T(8,128)S(1)} %constant_dynamic-slice_fusion), kind=kLoop, calls=%fused_computation.11 | loop fusion | flops 294912 | bytes 3538948 | tf_op jit(solution)/shard_map/jit(dynamic_update_index_in_dim)/dynamic_update_slice | solution.py:44
  106.1 1.2 convert_element_type.51
  107.3 1.8 %convert_bitcast_fusion.2 = bf16[1,1024,128]{2,1,0:T(8,128)(2,1)} fusion(f32[1024,128]{1,0:T(8,128)} %reduce-scatter.4.cloned.1.call-done), kind=kLoop, calls=%fused_computation.63 | loop fusion | flops 131072 | bytes 786432 | tf_op jit(solution)/shard_map/broadcast_in_dim | solution.py:84
  109.1 1.8 %convert_bitcast_fusion.1 = bf16[1,1024,128]{2,1,0:T(8,128)(2,1)} fusion(f32[1024,128]{1,0:T(8,128)} %reduce-scatter.6.cloned.1.call-done), kind=kLoop, calls=%fused_computation.62 | loop fusion | flops 131072 | bytes 786432 | tf_op jit(solution)/shard_map/broadcast_in_dim | solution.py:85
  110.9 20.7 %reduce-scatter.8.cloned.1.call-done = f32[128,1024]{1,0:T(8,128)} async-done(((f32[128,2048]{1,0:T(8,128)}), f32[128,1024]{1,0:T(8,128)}) %reduce-scatter.8.cloned.1.call-update) | async-done | bytes 524304 | tf_op jit(solution)/shard_map/reduce_scatter | solution.py:81
  131.5 1.8 %convert_bitcast_fusion = bf16[1,128,1024]{2,1,0:T(8,128)(2,1)} fusion(f32[128,1024]{1,0:T(8,128)} %reduce-scatter.8.cloned.1.call-done), kind=kLoop, calls=%fused_computation.61 | loop fusion | flops 131072 | bytes 786432 | tf_op jit(solution)/shard_map/broadcast_in_dim | solution.py:86
  (76 shorter events, 8.0 us)
Async XLA Ops:
  7.2 100.2 %reduce-scatter.4.cloned.1.call-start = ((), (), s32[]{:S(2)}) async-start(), calls=%async_computation.3 | async-start | bytes 1572864 | tf_op jit(solution)/shard_map/reduce_scatter | solution.py:79
  12.5 8.0 %copy-start.1 = (bf16[2,144,2048]{2,1,0:T(8,128)(2,1)S(1)}, bf16[2,144,2048]{2,1,0:T(8,128)(2,1)}, u32[]{:S(2)}) copy-start(bf16[2,144,2048]{2,1,0:T(8,128)(2,1)} %param.7) | copy-start | bytes 3538948
  15.0 10.4 %copy-start.12 = (bf16[1,1024,128]{2,1,0:T(8,128)(2,1)S(1)}, bf16[1,1024,128]{2,1,0:T(8,128)(2,1)}, u32[]{:S(2)}) copy-start(bf16[1,1024,128]{2,1,0:T(8,128)(2,1)} %param.8) | copy-start | bytes 786436
  15.0 36.2 %collective-permute-start = (bf16[144,2048]{1,0:T(8,128)(2,1)}, bf16[144,2048]{1,0:T(8,128)(2,1)S(1)}, u32[]{:S(2)}, u32[]{:S(2)}) collective-permute-start(bf16[144,2048]{1,0:T(8,128)(2,1)} %get-tuple-element.7), channel_id=1, source_target_pairs={{2,0},{4,2},{6,4},{8,6},{10,8},{12,10},{14,12},{16,14},{18,16},{20... | collective-permute-start | bytes 1769480 | tf_op jit(solution)/shard_map/ppermute | solution.py:12
  21.6 20.2 %copy-start = (bf16[2,144,2048]{2,1,0:T(8,128)(2,1)S(1)}, bf16[2,144,2048]{2,1,0:T(8,128)(2,1)}, u32[]{:S(2)}) copy-start(bf16[2,144,2048]{2,1,0:T(8,128)(2,1)} %param.6) | copy-start | bytes 3538948
  21.6 32.5 %collective-permute-start.1 = (bf16[144,2048]{1,0:T(8,128)(2,1)}, bf16[144,2048]{1,0:T(8,128)(2,1)}, u32[]{:S(2)}, u32[]{:S(2)}) collective-permute-start(bf16[144,2048]{1,0:T(8,128)(2,1)} %get-tuple-element.5), channel_id=1, source_target_pairs={{2,0},{4,2},{6,4},{8,6},{10,8},{12,10},{14,12},{16,14},{18,16},{20... | collective-permute-start | bytes 1769480 | tf_op jit(solution)/shard_map/ppermute | solution.py:12
  22.3 31.2 %collective-permute-start.2 = (bf16[144,2048]{1,0:T(8,128)(2,1)}, bf16[144,2048]{1,0:T(8,128)(2,1)S(1)}, u32[]{:S(2)}, u32[]{:S(2)}) collective-permute-start(bf16[144,2048]{1,0:T(8,128)(2,1)} %get-tuple-element.6), channel_id=1, source_target_pairs={{4,0},{6,2},{8,4},{10,6},{12,8},{14,10},{16,12},{18,14},{20,16},{2... | collective-permute-start | bytes 1769480 | tf_op jit(solution)/shard_map/ppermute | solution.py:12
  22.8 37.0 %collective-permute-start.3 = (bf16[144,2048]{1,0:T(8,128)(2,1)}, bf16[144,2048]{1,0:T(8,128)(2,1)}, u32[]{:S(2)}, u32[]{:S(2)}) collective-permute-start(bf16[144,2048]{1,0:T(8,128)(2,1)} %get-tuple-element.4), channel_id=1, source_target_pairs={{4,0},{6,2},{8,4},{10,6},{12,8},{14,10},{16,12},{18,14},{20,16},{2... | collective-permute-start | bytes 1769480 | tf_op jit(solution)/shard_map/ppermute | solution.py:12
  41.7 1.0 copy-start.13
  42.1 8.6 %copy-start.8 = (f32[144,128]{1,0:T(8,128)}, f32[144,128]{1,0:T(8,128)S(1)}, u32[]{:S(2)}) copy-start(f32[144,128]{1,0:T(8,128)S(1)} %fusion.10) | copy-start | bytes 221188
  42.1 7.7 %copy-start.2 = (bf16[2,144,2048]{2,1,0:T(8,128)(2,1)S(1)}, bf16[2,144,2048]{2,1,0:T(8,128)(2,1)}, u32[]{:S(2)}) copy-start(bf16[2,144,2048]{2,1,0:T(8,128)(2,1)} %param.7) | copy-start | bytes 3538948
  42.7 8.5 %copy-start.10 = (f32[144,128]{1,0:T(8,128)}, f32[144,128]{1,0:T(8,128)S(1)}, u32[]{:S(2)}) copy-start(f32[144,128]{1,0:T(8,128)S(1)} %fusion.12) | copy-start | bytes 221188
  50.7 0.8 copy-start.14
  53.8 6.0 %copy-start.4 = (f32[144,128]{1,0:T(8,128)}, f32[144,128]{1,0:T(8,128)S(1)}, u32[]{:S(2)}) copy-start(f32[144,128]{1,0:T(8,128)S(1)} %fusion.20) | copy-start | bytes 221188
  54.1 5.7 %copy-start.6 = (f32[144,128]{1,0:T(8,128)}, f32[144,128]{1,0:T(8,128)S(1)}, u32[]{:S(2)}) copy-start(f32[144,128]{1,0:T(8,128)S(1)} %fusion.28) | copy-start | bytes 221188
  61.8 0.6 copy-start.16
  63.9 45.2 %reduce-scatter.6.cloned.1.call-start = ((), (), s32[]{:S(2)}) async-start(), calls=%async_computation.4 | async-start | bytes 1572864 | tf_op jit(solution)/shard_map/reduce_scatter | solution.py:80
  64.0 1.3 copy-start.22
  65.3 0.8 copy-start.20
  66.1 1.6 %copy-start.3 = (bf16[2,144,2048]{2,1,0:T(8,128)(2,1)S(1)}, bf16[2,144,2048]{2,1,0:T(8,128)(2,1)}, u32[]{:S(2)}) copy-start(bf16[2,144,2048]{2,1,0:T(8,128)(2,1)} %param.7) | copy-start | bytes 3538948
  66.1 1.6 %copy-start.9 = (f32[144,128]{1,0:T(8,128)S(1)}, f32[144,128]{1,0:T(8,128)}, u32[]{:S(2)}) copy-start(f32[144,128]{1,0:T(8,128)} %copy-done.8) | copy-start | bytes 221188
  66.1 1.6 %copy-start.11 = (f32[144,128]{1,0:T(8,128)S(1)}, f32[144,128]{1,0:T(8,128)}, u32[]{:S(2)}) copy-start(f32[144,128]{1,0:T(8,128)} %copy-done.10) | copy-start | bytes 221188
  67.6 64.0 %reduce-scatter.8.cloned.1.call-start = ((), (), s32[]{:S(2)}) async-start(), calls=%async_computation.5 | async-start | bytes 1572864 | tf_op jit(solution)/shard_map/reduce_scatter | solution.py:81
  68.0 1.1 copy-start.19
  69.1 0.8 copy-start.23
  69.9 0.8 copy-start.17
  70.2 0.8 copy-start.21
  70.2 27.8 %collective-permute-start.4 = (f32[144,2048]{1,0:T(8,128)S(1)}, f32[144,2048]{1,0:T(8,128)}, u32[]{:S(2)}, u32[]{:S(2)}) collective-permute-start(f32[144,2048]{1,0:T(8,128)S(1)} %convolution_add_fusion.1), channel_id=1, source_target_pairs={{30,0},{0,2},{2,4},{4,6},{6,8},{8,10},{10,12},{12,14},{14,16},{16,... | collective-permute-start | bytes 3538952 | tf_op jit(solution)/shard_map/ppermute | solution.py:12
  72.3 1.8 %copy-start.5 = (f32[144,128]{1,0:T(8,128)S(1)}, f32[144,128]{1,0:T(8,128)}, u32[]{:S(2)}) copy-start(f32[144,128]{1,0:T(8,128)} %copy-done.4) | copy-start | bytes 221188
  72.3 1.8 %copy-start.7 = (f32[144,128]{1,0:T(8,128)S(1)}, f32[144,128]{1,0:T(8,128)}, u32[]{:S(2)}) copy-start(f32[144,128]{1,0:T(8,128)} %copy-done.6) | copy-start | bytes 221188
  72.3 32.4 %collective-permute-start.5 = (f32[144,2048]{1,0:T(8,128)}, f32[144,2048]{1,0:T(8,128)}, u32[]{:S(2)}, u32[]{:S(2)}) collective-permute-start(f32[144,2048]{1,0:T(8,128)} %convolution_add_fusion), channel_id=1, source_target_pairs={{28,0},{30,2},{0,4},{2,6},{4,8},{6,10},{8,12},{10,14},{12,16},{14,... | collective-permute-start | bytes 3538952 | tf_op jit(solution)/shard_map/ppermute | solution.py:12
  76.6 0.8 copy-start.15
  (1 other events, 0.6 us)
Sparse Core Ops, SparseCore 0:
  64.1 22.1 reduce-scatter.3
  88.6 20.3 reduce-scatter.5
  111.2 20.3 reduce-scatter.7
where the time goes:
time: 141 us; the launch traced here: 140 us
  waiting for transfers between devices  50.8 us (36%)
  blocking collectives  22.6 us (16%)
  matrix products  20.4 us (14%)
  between operations  20 us (14%)
  other arithmetic  9.4 us (7%)
  starting transfers between devices  8.54 us (6%)
  local copies, waits for them, and re-layouts  8.08 us (6%)
    ppermute x6, waiting for transfers between devices, shifted(): return lax.ppermute(block, axis, route)  30.1 us
    reduce_scatter x1, waiting for transfers between devices, on_device(): lax.psum_scatter(sums[2], 'dp', scatter_dimension=1, tiled=True)  20.7 us
    ppermute x6, starting transfers between devices, shifted(): return lax.ppermute(block, axis, route)  8.42 us
    all_gather x1, blocking collectives, on_device(): lax.all_gather(w_gate, 'dp', axis=1, tiled=True)  8.16 us
    all_gather x1, blocking collectives, on_device(): lax.all_gather(w_up, 'dp', axis=1, tiled=True)  7.44 us
    all_gather x1, blocking collectives, on_device(): lax.all_gather(w_down, 'dp', axis=2, tiled=True)  7.04 us
    dot_general x3, matrix products, slab_terms(): lax.dot_general(rows_g, w_down, by_units, preferred_element_type=jnp.floa...  4.98 us
    dot_general x3, matrix products, slab_terms(): lax.dot_general(hidden, rows_g, by_rows, preferred_element_type=jnp.float32)  4.21 us
  transfers between devices with their start and end apart: 9, of which 5 were waited for; matrix products, arithmetic and copies ran while one was open for 19% of the time, Pallas kernels for 0%

commit v1 on v0

v1 whole, which is shorter than its diff:
```python
import functools

import jax
import jax.numpy as jnp
from jax import lax
from jax.experimental import pallas as pl
from jax.experimental.pallas import tpu as pltpu
from jax.sharding import PartitionSpec as P

TICKS = 3
MESH = pl.DeviceIdType.MESH
F32 = jnp.float32
BF16 = jnp.bfloat16


def dot(a, b, ca, cb):
    return lax.dot_general(a, b, (((ca,), (cb,)), ((), ())), preferred_element_type=F32)


def kernel(
    n, layers,
    layer_ref, acts, cot, wg, wu, wd,
    gg, gu, gd, ag,
    wgu, wdn, stage, rows, ret_out, ret_in, ag0, acc, accd,
    gs, gsd, gr, grd,
    send_sem, recv_sem,
):
    b = lax.axis_index("blk")
    r = lax.axis_index("dp")
    o = 1 - r
    unit = wg.shape[2]
    half = wg.shape[1]

    def at(k):
        return lax.rem(b + k + n, n)

    barrier = pltpu.get_barrier_semaphore()
    pl.semaphore_signal(barrier, inc=1, device_id=(b, o), device_id_type=MESH)
    for k in range(1, TICKS):
        pl.semaphore_signal(barrier, inc=1, device_id=(at(k), r), device_id_type=MESH)
        pl.semaphore_signal(barrier, inc=1, device_id=(at(-k), r), device_id_type=MESH)

    count = [0]

    def copy(src, dst, dev):
        i = count[0]
        count[0] += 1
        return pltpu.make_async_remote_copy(
            src_ref=src, dst_ref=dst, send_sem=send_sem.at[i], recv_sem=recv_sem.at[i],
            device_id=dev, device_id_type=MESH,
        )

    layer = [layer_ref[at(-k)] for k in range(TICKS)]
    for k in range(1, TICKS):
        stage[k - 1, 0] = acts[layer[k]]
        stage[k - 1, 1] = cot[layer[k]]
    pl.semaphore_wait(barrier, 2 * TICKS - 1)

    weights = [
        copy(wg.at[0], wgu.at[r, :, pl.ds(0, unit)], (b, o)),
        copy(wu.at[0], wgu.at[r, :, pl.ds(unit, unit)], (b, o)),
        copy(wd.at[0], wdn.at[r], (b, o)),
    ]
    tokens = [copy(stage.at[k], rows.at[k], (at(-k - 1), r)) for k in range(TICKS - 1)]
    tokens[0].start()
    for c in weights:
        c.start()
    for c in tokens[1:]:
        c.start()
    wgu[r, :, 0:unit] = wg[0]
    wgu[r, :, unit : 2 * unit] = wu[0]
    wdn[r] = wd[0]

    def meet(k, x, g):
        both = dot(x[:, :half], wgu[0], 1, 0) + dot(x[:, half:], wgu[1], 1, 0)
        hg = dot(g[:, :half], wdn[0], 1, 1) + dot(g[:, half:], wdn[1], 1, 1)
        gate, up = both[:, :unit], both[:, unit:]
        sig = jax.nn.sigmoid(gate)
        act = gate * sig
        hidden = (act * up).astype(BF16)
        up_in = (hg * act).astype(BF16)
        gate_in = (hg * up * sig * (1.0 + gate * (1.0 - sig))).astype(BF16)
        pair = jnp.concatenate([gate_in, up_in], axis=1)
        return hidden, pair

    def grads(k, x, g, hidden, pair):
        for h in range(2):
            t = dot(x[:, h * half : (h + 1) * half], pair, 0, 0)
            d = dot(hidden, g[:, h * half : (h + 1) * half], 0, 0)
            if k == 0:
                acc[h] = t
                accd[h] = d
            else:
                acc[h] = acc[h] + t
                accd[h] = accd[h] + d

    for c in weights:
        c.wait_recv()
    x, g = acts[layer[0]], cot[layer[0]]
    hidden, pair = meet(0, x, g)
    for h in range(2):
        ag0[:, h * half : (h + 1) * half] = dot(pair, wgu[h], 1, 1)
    grads(0, x, g, hidden, pair)

    returns = []
    for k in range(1, TICKS):
        tokens[k - 1].wait_recv()
        x, g = rows[k - 1, 0], rows[k - 1, 1]
        hidden, pair = meet(k, x, g)
        for h in range(2):
            ret_out[k - 1, :, h * half : (h + 1) * half] = dot(pair, wgu[h], 1, 1).astype(BF16)
        back = copy(ret_out.at[k - 1], ret_in.at[k - 1], (at(k), r))
        back.start()
        returns.append(back)
        grads(k, x, g, hidden, pair)

    gs[...] = acc[o].astype(BF16)
    gsd[...] = accd[o].astype(BF16)
    halves = [copy(gs, gr, (b, o)), copy(gsd, grd, (b, o))]
    for c in halves:
        c.start()

    for c in returns:
        c.wait_recv()
    for l in range(layers):
        total = jnp.where(layer[0] == l, 1.0, 0.0) * ag0[...]
        for k in range(1, TICKS):
            total += jnp.where(layer[k] == l, 1.0, 0.0) * ret_in[k - 1].astype(F32)
        ag[l] = total.astype(BF16)

    for c in halves:
        c.wait_recv()
    gg[0] = (acc[r, :, :unit] + gr[:, :unit].astype(F32)).astype(BF16)
    gu[0] = (acc[r, :, unit:] + gr[:, unit:].astype(F32)).astype(BF16)
    gd[0] = (accd[r] + grd[...].astype(F32)).astype(BF16)
    for c in weights + tokens + returns + halves:
        c.wait_send()


def on_device(n, acts, cotangent, w_gate, w_up, w_down, slab_layer):
    layers, tok, width = acts.shape
    half, unit = w_gate.shape[1:]
    vmem = pl.BlockSpec(memory_space=pltpu.VMEM)
    copies = 3 + 2 * (TICKS - 1) + 2
    return pl.pallas_call(
        functools.partial(kernel, n, layers),
        out_shape=(
            jax.ShapeDtypeStruct(w_gate.shape, BF16),
            jax.ShapeDtypeStruct(w_up.shape, BF16),
            jax.ShapeDtypeStruct(w_down.shape, BF16),
            jax.ShapeDtypeStruct(acts.shape, BF16),
        ),
        in_specs=[pl.BlockSpec(memory_space=pltpu.SMEM)] + [vmem] * 5,
        out_specs=(vmem,) * 4,
        scratch_shapes=[
            pltpu.VMEM((2, half, 2 * unit), BF16),
            pltpu.VMEM((2, unit, half), BF16),
            pltpu.VMEM((TICKS - 1, 2, tok, width), BF16),
            pltpu.VMEM((TICKS - 1, 2, tok, width), BF16),
            pltpu.VMEM((TICKS - 1, tok, width), BF16),
            pltpu.VMEM((TICKS - 1, tok, width), BF16),
            pltpu.VMEM((tok, width), F32),
            pltpu.VMEM((2, half, 2 * unit), F32),
            pltpu.VMEM((2, unit, half), F32),
            pltpu.VMEM((half, 2 * unit), BF16),
            pltpu.VMEM((unit, half), BF16),
            pltpu.VMEM((half, 2 * unit), BF16),
            pltpu.VMEM((unit, half), BF16),
            pltpu.SemaphoreType.DMA((copies,)),
            pltpu.SemaphoreType.DMA((copies,)),
        ],
        compiler_params=pltpu.CompilerParams(
            collective_id=0, has_side_effects=True, vmem_limit_bytes=48 * 1024 * 1024
        ),
    )(slab_layer, acts, cotangent, w_gate, w_up, w_down)


def solution(mesh):
    in_specs = (
        P(None, ("blk", "dp"), None),
        P(None, ("blk", "dp"), None),
        P("blk", "dp", None),
        P("blk", "dp", None),
        P("blk", None, "dp"),
        P(),
    )
    out_specs = (
        P("blk", "dp", None),
        P("blk", "dp", None),
        P("blk", None, "dp"),
        P(None, ("blk", "dp"), None),
    )
    return jax.shard_map(
        functools.partial(on_device, mesh.shape["blk"]),
        mesh=mesh, in_specs=in_specs, out_specs=out_specs, check_vma=False,
    )
```

time: 141 us -> 86.4 us (0.61)
  Pallas kernels: 0 us -> 76.3 us
  waiting for transfers between devices: 50.8 us -> 0 us
  blocking collectives: 22.6 us -> 0 us
  matrix products: 20.4 us -> 0 us
  between operations: 20 us -> 0.66 us
  other arithmetic: 9.4 us -> 0 us
  starting transfers between devices: 8.54 us -> 0 us
    pallas_call x0 -> x1, Pallas kernels: none -> 76.3 us  [on_device(): pl.pallas_call(functools.partial(kernel, n, layers), out_shape=(jax.Shape...]
    ppermute x6 -> x0, waiting for transfers between devices: 30.1 us -> none  [shifted(): return lax.ppermute(block, axis, route)]
    all_gather x3 -> x0, blocking collectives: 22.6 us -> none  [the longest x1 8.16 us: on_device(): lax.all_gather(w_gate, 'dp', axis=1, tiled=True)]
    reduce_scatter x3 -> x0, waiting for transfers between devices: 20.7 us -> none  [the longest x1 20.7 us: on_device(): lax.psum_scatter(sums[2], 'dp', scatter_dimension=1, tiled=True)]
    dot_general x24 -> x0, matrix products: 20.4 us -> none  [the longest x3 4.98 us: slab_terms(): lax.dot_general(rows_g, w_down, by_units, preferred_element_type=jnp.floa...]
    ppermute x6 -> x0, starting transfers between devices: 8.42 us -> none  [shifted(): return lax.ppermute(block, axis, route)]
    unnamed x48 -> x16, local copies, waits for them, and re-layouts: 2.67 us -> 9.16 us
    broadcast_in_dim x3 -> x0, other arithmetic: 5.32 us -> none  [the longest x1 1.78 us: on_device(): halves[2].astype(jnp.bfloat16)[None]]
  transfers between devices with their start and end apart: 9 -> 0, of which waited for: 5 -> 0; matrix products, arithmetic and copies ran while one was open for 19% -> 0% of each run, Pallas kernels for 0% -> 0%
where the time goes in v1:
time: 86.4 us; the launch traced here: 86.1 us
  Pallas kernels  76.3 us (88%)
  local copies, waits for them, and re-layouts  9.16 us (11%)
    pallas_call x1, Pallas kernels, on_device(): pl.pallas_call(functools.partial(kernel, n, layers), out_shape=(jax.Shape...  76.3 us
    unnamed x16, local copies, waits for them, and re-layouts  9.16 us

profile of v1, /device:TPU:0, one launch (start us, length us, event | category | flops | bytes accessed | tf_op | source)
XLA Modules:
  0.0 86.1 jit_solution(893968258102875436)
XLA Ops:
  0.6 0.0 copy-start
  0.6 1.3 %copy-done = bf16[2,144,2048]{2,1,0:T(8,128)(2,1)S(1)} copy-done((bf16[2,144,2048]{2,1,0:T(8,128)(2,1)S(1)}, bf16[2,144,2048]{2,1,0:T(8,128)(2,1)}, u32[]{:S(2)}) %copy-start) | copy-done | bytes 1179672
  1.9 0.0 copy-start.1
  1.9 1.3 %copy-done.1 = bf16[2,144,2048]{2,1,0:T(8,128)(2,1)S(1)} copy-done((bf16[2,144,2048]{2,1,0:T(8,128)(2,1)S(1)}, bf16[2,144,2048]{2,1,0:T(8,128)(2,1)}, u32[]{:S(2)}) %copy-start.1) | copy-done | bytes 1179672
  3.2 0.0 copy-start.2
  3.2 0.9 %copy-done.2 = bf16[1,1024,128]{2,1,0:T(8,128)(2,1)S(1)} copy-done((bf16[1,1024,128]{2,1,0:T(8,128)(2,1)S(1)}, bf16[1,1024,128]{2,1,0:T(8,128)(2,1)}, u32[]{:S(2)}) %copy-start.2) | copy-done | bytes 262168
  4.1 0.0 copy-start.3
  4.1 0.9 %copy-done.3 = bf16[1,1024,128]{2,1,0:T(8,128)(2,1)S(1)} copy-done((bf16[1,1024,128]{2,1,0:T(8,128)(2,1)S(1)}, bf16[1,1024,128]{2,1,0:T(8,128)(2,1)}, u32[]{:S(2)}) %copy-start.3) | copy-done | bytes 262168
  5.1 0.0 copy-start.4
  5.1 0.9 %copy-done.4 = bf16[1,128,1024]{2,1,0:T(8,128)(2,1)S(1)} copy-done((bf16[1,128,1024]{2,1,0:T(8,128)(2,1)S(1)}, bf16[1,128,1024]{2,1,0:T(8,128)(2,1)}, u32[]{:S(2)}) %copy-start.4) | copy-done | bytes 262168
  6.0 0.0 copy-start.5
  6.0 0.7 copy-done.5
  6.7 76.3 %shard_map.93 = (bf16[1,1024,128]{2,1,0:T(8,128)(2,1)S(1)}, bf16[1,1024,128]{2,1,0:T(8,128)(2,1)S(1)}, bf16[1,128,1024]{2,1,0:T(8,128)(2,1)S(1)}, bf16[2,144,2048]{2,1,0:T(8,128)(2,1)S(1)}) custom-call(s32[16]{0:T(128)S(1)} %copy-done.5, bf16[2,144,2048]{2,1,0:T(8,128)(2,1)S(1)} %copy-done, bf16[2,144,2048]{2,1,0:T(8,128)(2,1)S(1)} %copy-done.1, ...), custom_call_target="tpu_custom_call" | custom-call | tf_op jit(solution)/shard_map/pallas_call | solution.py:145
  83.0 0.7 copy.14
  83.7 0.7 copy.15
  84.4 0.7 copy.16
  85.1 1.0 %copy.17 = bf16[2,144,2048]{2,1,0:T(8,128)(2,1)} copy(bf16[2,144,2048]{2,1,0:T(8,128)(2,1)S(1)} %get-tuple-element.11) | data formatting | bytes 2359296
Async XLA Ops:
  0.6 1.3 %copy-start = (bf16[2,144,2048]{2,1,0:T(8,128)(2,1)S(1)}, bf16[2,144,2048]{2,1,0:T(8,128)(2,1)}, u32[]{:S(2)}) copy-start(bf16[2,144,2048]{2,1,0:T(8,128)(2,1)} %acts.1) | copy-start | bytes 3538948
  1.9 1.3 %copy-start.1 = (bf16[2,144,2048]{2,1,0:T(8,128)(2,1)S(1)}, bf16[2,144,2048]{2,1,0:T(8,128)(2,1)}, u32[]{:S(2)}) copy-start(bf16[2,144,2048]{2,1,0:T(8,128)(2,1)} %cot.1) | copy-start | bytes 3538948
  3.2 0.9 %copy-start.2 = (bf16[1,1024,128]{2,1,0:T(8,128)(2,1)S(1)}, bf16[1,1024,128]{2,1,0:T(8,128)(2,1)}, u32[]{:S(2)}) copy-start(bf16[1,1024,128]{2,1,0:T(8,128)(2,1)} %wg.1) | copy-start | bytes 786436
  4.1 0.9 %copy-start.3 = (bf16[1,1024,128]{2,1,0:T(8,128)(2,1)S(1)}, bf16[1,1024,128]{2,1,0:T(8,128)(2,1)}, u32[]{:S(2)}) copy-start(bf16[1,1024,128]{2,1,0:T(8,128)(2,1)} %wu.1) | copy-start | bytes 786436
  5.1 0.9 %copy-start.4 = (bf16[1,128,1024]{2,1,0:T(8,128)(2,1)S(1)}, bf16[1,128,1024]{2,1,0:T(8,128)(2,1)}, u32[]{:S(2)}) copy-start(bf16[1,128,1024]{2,1,0:T(8,128)(2,1)} %wd.1) | copy-start | bytes 786436
  6.0 0.7 copy-start.5

commit v2 on v1

--- a/solution.py
+++ b/solution.py
@@ -19,11 +19,11 @@
 
 def kernel(
     n, layers,
-    layer_ref, acts, cot, wg, wu, wd,
+    layer_ref, acts_hbm, cot_hbm, wg, wu, wd,
     gg, gu, gd, ag,
-    wgu, wdn, stage, rows, ret_out, ret_in, ag0, acc, accd,
+    acts, cot, wgu, wdn, own, stage, rows, ret_out, ret_in, ag0, acc, accd,
     gs, gsd, gr, grd,
-    send_sem, recv_sem,
+    send_sem, recv_sem, load_sem,
 ):
     b = lax.axis_index("blk")
     r = lax.axis_index("dp")
@@ -34,6 +34,18 @@
     def at(k):
         return lax.rem(b + k + n, n)
 
+    loads = [
+        pltpu.make_async_copy(src, dst, load_sem.at[i])
+        for i, (src, dst) in enumerate([
+            (acts_hbm, acts),
+            (cot_hbm, cot),
+            (wg.at[0], wgu.at[r, :, pl.ds(0, unit)]),
+            (wu.at[0], wgu.at[r, :, pl.ds(unit, unit)]),
+            (wd.at[0], wdn.at[r]),
+        ])
+    ]
+    for c in loads:
+        c.start()
     barrier = pltpu.get_barrier_semaphore()
     pl.semaphore_signal(barrier, inc=1, device_id=(b, o), device_id_type=MESH)
     for k in range(1, TICKS):
@@ -51,9 +63,6 @@
         )
 
     layer = [layer_ref[at(-k)] for k in range(TICKS)]
-    for k in range(1, TICKS):
-        stage[k - 1, 0] = acts[layer[k]]
-        stage[k - 1, 1] = cot[layer[k]]
     pl.semaphore_wait(barrier, 2 * TICKS - 1)
 
     weights = [
@@ -62,14 +71,18 @@
         copy(wd.at[0], wdn.at[r], (b, o)),
     ]
     tokens = [copy(stage.at[k], rows.at[k], (at(-k - 1), r)) for k in range(TICKS - 1)]
-    tokens[0].start()
     for c in weights:
         c.start()
-    for c in tokens[1:]:
-        c.start()
-    wgu[r, :, 0:unit] = wg[0]
-    wgu[r, :, unit : 2 * unit] = wu[0]
-    wdn[r] = wd[0]
+    for c in loads[:2]:
+        c.wait()
+    for k in range(TICKS - 1, 0, -1):
+        stage[k - 1, 0] = acts[layer[k]]
+        stage[k - 1, 1] = cot[layer[k]]
+        tokens[k - 1].start()
+    own[0] = acts[layer[0]]
+    own[1] = cot[layer[0]]
+    for c in loads[2:]:
+        c.wait()
 
     def meet(k, x, g):
         both = dot(x[:, :half], wgu[0], 1, 0) + dot(x[:, half:], wgu[1], 1, 0)
@@ -83,42 +96,52 @@
         pair = jnp.concatenate([gate_in, up_in], axis=1)
         return hidden, pair
 
-    def grads(k, x, g, hidden, pair):
+    def cut(v, h):
+        return v[:, pl.ds(pl.multiple_of(h * half, half), half)]
+
+    def grads(h, parts):
+        t = sum(dot(cut(x, h)[...], pair, 0, 0) for x, g, hidden, pair in parts)
+        d = sum(dot(hidden, cut(g, h)[...], 0, 0) for x, g, hidden, pair in parts)
+        return t, d
+
+    def back(dst, k, pair):
         for h in range(2):
-            t = dot(x[:, h * half : (h + 1) * half], pair, 0, 0)
-            d = dot(hidden, g[:, h * half : (h + 1) * half], 0, 0)
-            if k == 0:
-                acc[h] = t
-                accd[h] = d
-            else:
-                acc[h] = acc[h] + t
-                accd[h] = accd[h] + d
+            dst[:, h * half : (h + 1) * half] = dot(pair, wgu[h], 1, 1).astype(dst.dtype)
 
     for c in weights:
         c.wait_recv()
-    x, g = acts[layer[0]], cot[layer[0]]
-    hidden, pair = meet(0, x, g)
+    hidden, pair = meet(0, own.at[0], own.at[1])
+    back(ag0, 0, pair)
     for h in range(2):
-        ag0[:, h * half : (h + 1) * half] = dot(pair, wgu[h], 1, 1)
-    grads(0, x, g, hidden, pair)
-
-    returns = []
-    for k in range(1, TICKS):
+        acc[h], accd[h] = grads(h, [(own.at[0], own.at[1], hidden, pair)])
+
+    for c in tokens[1:]:
+        c.wait_send()
+    returns = [copy(ret_out.at[k], ret_in.at[k], (at(k + 1), r)) for k in range(TICKS - 1)]
+    for k in range(TICKS - 1, 0, -1):
         tokens[k - 1].wait_recv()
-        x, g = rows[k - 1, 0], rows[k - 1, 1]
+        x, g = rows.at[k - 1, 0], rows.at[k - 1, 1]
         hidden, pair = meet(k, x, g)
-        for h in range(2):
-            ret_out[k - 1, :, h * half : (h + 1) * half] = dot(pair, wgu[h], 1, 1).astype(BF16)
-        back = copy(ret_out.at[k - 1], ret_in.at[k - 1], (at(k), r))
-        back.start()
-        returns.append(back)
-        grads(k, x, g, hidden, pair)
-
-    gs[...] = acc[o].astype(BF16)
-    gsd[...] = accd[o].astype(BF16)
+        if k > 1:
+            back(ret_out.at[k - 1], k, pair)
+            for h in range(2):
+                t, d = grads(h, [(x, g, hidden, pair)])
+                acc[h] += t
+                accd[h] += d
+    t, d = grads(o, [(x, g, hidden, pair)])
+    gs[...] = (acc[o] + t).astype(BF16)
+    gsd[...] = (accd[o] + d).astype(BF16)
     halves = [copy(gs, gr, (b, o)), copy(gsd, grd, (b, o))]
     for c in halves:
         c.start()
+    tokens[0].wait_send()
+    for c in returns[1:]:
+        c.start()
+    back(ret_out.at[0], 1, pair)
+    returns[0].start()
+    t, d = grads(r, [(x, g, hidden, pair)])
+    acc[r] += t
+    accd[r] += d
 
     for c in returns:
         c.wait_recv()
@@ -133,8 +156,23 @@
     gg[0] = (acc[r, :, :unit] + gr[:, :unit].astype(F32)).astype(BF16)
     gu[0] = (acc[r, :, unit:] + gr[:, unit:].astype(F32)).astype(BF16)
     gd[0] = (accd[r] + grd[...].astype(F32)).astype(BF16)
-    for c in weights + tokens + returns + halves:
+    for c in weights + returns + halves:
         c.wait_send()
+
+
+def place(*refs):
+    count = len(refs) // 3
+    sems = refs[-1]
+    bufs = refs[2 * count : 3 * count]
+    ins = [pltpu.make_async_copy(refs[i], bufs[i], sems.at[i]) for i in range(count)]
+    outs = [pltpu.make_async_copy(bufs[i], refs[count + i], sems.at[i]) for i in range(count)]
+    for c in ins:
+        c.start()
+    for i in range(count):
+        ins[i].wait()
+        outs[i].start()
+    for c in outs:
+        c.wait()
 
 
 def on_device(n, acts, cotangent, w_gate, w_up, w_down, slab_layer):
@@ -142,7 +180,7 @@
     half, unit = w_gate.shape[1:]
     vmem = pl.BlockSpec(memory_space=pltpu.VMEM)
     copies = 3 + 2 * (TICKS - 1) + 2
-    return pl.pallas_call(
+    found = pl.pallas_call(
         functools.partial(kernel, n, layers),
         out_shape=(
             jax.ShapeDtypeStruct(w_gate.shape, BF16),
@@ -150,11 +188,14 @@
             jax.ShapeDtypeStruct(w_down.shape, BF16),
             jax.ShapeDtypeStruct(acts.shape, BF16),
         ),
-        in_specs=[pl.BlockSpec(memory_space=pltpu.SMEM)] + [vmem] * 5,
+        in_specs=[pl.BlockSpec(memory_space=pltpu.SMEM)] + [pl.BlockSpec(memory_space=pltpu.HBM)] * 5,
         out_specs=(vmem,) * 4,
         scratch_shapes=[
+            pltpu.VMEM(acts.shape, BF16),
+            pltpu.VMEM(acts.shape, BF16),
             pltpu.VMEM((2, half, 2 * unit), BF16),
             pltpu.VMEM((2, unit, half), BF16),
+            pltpu.VMEM((2, tok, width), BF16),
             pltpu.VMEM((TICKS - 1, 2, tok, width), BF16),
             pltpu.VMEM((TICKS - 1, 2, tok, width), BF16),
             pltpu.VMEM((TICKS - 1, tok, width), BF16),
@@ -168,11 +209,21 @@
             pltpu.VMEM((unit, half), BF16),
             pltpu.SemaphoreType.DMA((copies,)),
             pltpu.SemaphoreType.DMA((copies,)),
+            pltpu.SemaphoreType.DMA((5,)),
         ],
         compiler_params=pltpu.CompilerParams(
-            collective_id=0, has_side_effects=True, vmem_limit_bytes=48 * 1024 * 1024
+            collective_id=0, has_side_effects=True, vmem_limit_bytes=66_000_000
         ),
     )(slab_layer, acts, cotangent, w_gate, w_up, w_down)
+    hbm = pl.BlockSpec(memory_space=pltpu.HBM)
+    return pl.pallas_call(
+        place,
+        out_shape=tuple(jax.ShapeDtypeStruct(v.shape, v.dtype) for v in found),
+        in_specs=[hbm] * len(found),
+        out_specs=(hbm,) * len(found),
+        scratch_shapes=[pltpu.VMEM(v.shape, v.dtype) for v in found]
+        + [pltpu.SemaphoreType.DMA((len(found),))],
+    )(*found)
 
 
 def solution(mesh):

time: 86.4 us -> 72.6 us (0.84)
  local copies, waits for them, and re-layouts: 9.16 us -> 0 us
  Pallas kernels: 76.3 us -> 71.8 us
    unnamed x16 -> x0, local copies, waits for them, and re-layouts: 9.16 us -> none
    pallas_call x1, Pallas kernels: 76.3 us -> 69.3 us  [on_device(): pl.pallas_call(functools.partial(kernel, n, layers), out_shape=(jax.Shape...]
    pallas_call x0 -> x1, Pallas kernels: none -> 2.57 us  [on_device(): pl.pallas_call(place, out_shape=tuple((jax.ShapeDtypeStruct(v.shape, v.dt...]
where the time goes in v2:
time: 72.6 us; the launch traced here: 72.5 us
  Pallas kernels  71.8 us (99%)
    pallas_call x1, Pallas kernels, on_device(): pl.pallas_call(functools.partial(kernel, n, layers), out_shape=(jax.Shape...  69.3 us
    pallas_call x1, Pallas kernels, on_device(): pl.pallas_call(place, out_shape=tuple((jax.ShapeDtypeStruct(v.shape, v.dt...  2.57 us

profile of v2, /device:TPU:0, one launch (start us, length us, event | category | flops | bytes accessed | tf_op | source)
XLA Modules:
  0.0 72.5 jit_solution(12242706738139769572)
XLA Ops:
  0.6 69.3 %shard_map.93 = (bf16[1,1024,128]{2,1,0:T(8,128)(2,1)}, bf16[1,1024,128]{2,1,0:T(8,128)(2,1)}, bf16[1,128,1024]{2,1,0:T(8,128)(2,1)}, bf16[2,144,2048]{2,1,0:T(8,128)(2,1)}) custom-call(s32[16]{0:T(128)} %layer_ref.1, bf16[2,144,2048]{2,1,0:T(8,128)(2,1)} %acts_hbm.1, bf16[2,144,2048]{2,1,0:T(8,128)(2,1)} %cot_hbm.1, bf16[1,1024,128]{2,1,0:T(8,128)(2,1)} %wg.1, ...), custom_call_target="tpu_custom_call" | custom-call | tf_op jit(solution)/shard_map/pallas_call | solution.py:183
  69.9 2.6 %shard_map.94 = (bf16[1,1024,128]{2,1,0:T(8,128)(2,1)}, bf16[1,1024,128]{2,1,0:T(8,128)(2,1)}, bf16[1,128,1024]{2,1,0:T(8,128)(2,1)}, bf16[2,144,2048]{2,1,0:T(8,128)(2,1)}) custom-call(bf16[1,1024,128]{2,1,0:T(8,128)(2,1)} %get-tuple-element.8.refs_0_, bf16[1,1024,128]{2,1,0:T(8,128)(2,1)} %get-tuple-element.9.refs_1_, ...), custom_call_target="tpu_custom_call" | custom-call | tf_op jit(solution)/shard_map/pallas_call | solution.py:219

commit v3 on v2

--- a/solution.py
+++ b/solution.py
@@ -20,10 +20,11 @@
 def kernel(
     n, layers,
     layer_ref, acts_hbm, cot_hbm, wg, wu, wd,
+    gg_hbm, gu_hbm, gd_hbm, ag_hbm,
     gg, gu, gd, ag,
     acts, cot, wgu, wdn, own, stage, rows, ret_out, ret_in, ag0, acc, accd,
     gs, gsd, gr, grd,
-    send_sem, recv_sem, load_sem,
+    send_sem, recv_sem, load_sem, out_sem,
 ):
     b = lax.axis_index("blk")
     r = lax.axis_index("dp")
@@ -117,7 +118,8 @@
 
     for c in tokens[1:]:
         c.wait_send()
-    returns = [copy(ret_out.at[k], ret_in.at[k], (at(k + 1), r)) for k in range(TICKS - 1)]
+    returns = [copy(ret_out.at[k], ret_in.at[k], (at(k + 1), r)) for k in range(1, TICKS - 1)]
+    last = []
     for k in range(TICKS - 1, 0, -1):
         tokens[k - 1].wait_recv()
         x, g = rows.at[k - 1, 0], rows.at[k - 1, 1]
@@ -128,35 +130,51 @@
                 t, d = grads(h, [(x, g, hidden, pair)])
                 acc[h] += t
                 accd[h] += d
-    t, d = grads(o, [(x, g, hidden, pair)])
-    gs[...] = (acc[o] + t).astype(BF16)
-    gsd[...] = (accd[o] + d).astype(BF16)
     halves = [copy(gs, gr, (b, o)), copy(gsd, grd, (b, o))]
-    for c in halves:
-        c.start()
+    gs[...] = (acc[o] + dot(cut(x, o)[...], pair, 0, 0)).astype(BF16)
+    halves[0].start()
+    gsd[...] = (accd[o] + dot(hidden, cut(g, o)[...], 0, 0)).astype(BF16)
+    halves[1].start()
     tokens[0].wait_send()
-    for c in returns[1:]:
-        c.start()
-    back(ret_out.at[0], 1, pair)
-    returns[0].start()
+    for c in returns:
+        c.start()
+    for h in range(2):
+        side = pl.ds(h * half, half)
+        ret_out[0, :, side] = dot(pair, wgu[h], 1, 1).astype(BF16)
+        piece = copy(ret_out.at[0, :, side], ret_in.at[0, :, side], (at(1), r))
+        piece.start()
+        last.append(piece)
     t, d = grads(r, [(x, g, hidden, pair)])
     acc[r] += t
     accd[r] += d
 
-    for c in returns:
+    for c in returns + last:
         c.wait_recv()
+    puts = []
+
+    def put(src, dst):
+        c = pltpu.make_async_copy(src, dst, out_sem.at[len(puts)])
+        c.start()
+        puts.append(c)
+
     for l in range(layers):
         total = jnp.where(layer[0] == l, 1.0, 0.0) * ag0[...]
         for k in range(1, TICKS):
             total += jnp.where(layer[k] == l, 1.0, 0.0) * ret_in[k - 1].astype(F32)
         ag[l] = total.astype(BF16)
+        put(ag.at[l], ag_hbm.at[l])
 
     for c in halves:
         c.wait_recv()
     gg[0] = (acc[r, :, :unit] + gr[:, :unit].astype(F32)).astype(BF16)
+    put(gg, gg_hbm)
     gu[0] = (acc[r, :, unit:] + gr[:, unit:].astype(F32)).astype(BF16)
+    put(gu, gu_hbm)
     gd[0] = (accd[r] + grd[...].astype(F32)).astype(BF16)
-    for c in weights + returns + halves:
+    put(gd, gd_hbm)
+    for c in puts:
+        c.wait()
+    for c in weights + returns + last + halves:
         c.wait_send()
 
 
@@ -178,8 +196,7 @@
 def on_device(n, acts, cotangent, w_gate, w_up, w_down, slab_layer):
     layers, tok, width = acts.shape
     half, unit = w_gate.shape[1:]
-    vmem = pl.BlockSpec(memory_space=pltpu.VMEM)
-    copies = 3 + 2 * (TICKS - 1) + 2
+    copies = 3 + 2 * (TICKS - 1) + 1 + 2
     found = pl.pallas_call(
         functools.partial(kernel, n, layers),
         out_shape=(
@@ -189,8 +206,12 @@
             jax.ShapeDtypeStruct(acts.shape, BF16),
         ),
         in_specs=[pl.BlockSpec(memory_space=pltpu.SMEM)] + [pl.BlockSpec(memory_space=pltpu.HBM)] * 5,
-        out_specs=(vmem,) * 4,
+        out_specs=(pl.BlockSpec(memory_space=pltpu.HBM),) * 4,
         scratch_shapes=[
+            pltpu.VMEM(w_gate.shape, BF16),
+            pltpu.VMEM(w_up.shape, BF16),
+            pltpu.VMEM(w_down.shape, BF16),
+            pltpu.VMEM(acts.shape, BF16),
             pltpu.VMEM(acts.shape, BF16),
             pltpu.VMEM(acts.shape, BF16),
             pltpu.VMEM((2, half, 2 * unit), BF16),
@@ -210,6 +231,7 @@
             pltpu.SemaphoreType.DMA((copies,)),
             pltpu.SemaphoreType.DMA((copies,)),
             pltpu.SemaphoreType.DMA((5,)),
+            pltpu.SemaphoreType.DMA((layers + 3,)),
         ],
         compiler_params=pltpu.CompilerParams(
             collective_id=0, has_side_effects=True, vmem_limit_bytes=66_000_000

time: 72.6 us -> 72.3 us (level)
  no operation moved by 1% of the time
where the time goes in v3:
time: 72.3 us; the launch traced here: 72.2 us
  Pallas kernels  71.5 us (99%)
    pallas_call x1, Pallas kernels, on_device(): pl.pallas_call(functools.partial(kernel, n, layers), out_shape=(jax.Shape...  69 us
    pallas_call x1, Pallas kernels, on_device(): pl.pallas_call(place, out_shape=tuple((jax.ShapeDtypeStruct(v.shape, v.dt...  2.57 us

profile of v3, /device:TPU:0, one launch (start us, length us, event | category | flops | bytes accessed | tf_op | source)
XLA Modules:
  0.0 72.2 jit_solution(11301762298809448661)
XLA Ops:
  0.6 69.0 %shard_map.93 = (bf16[1,1024,128]{2,1,0:T(8,128)(2,1)}, bf16[1,1024,128]{2,1,0:T(8,128)(2,1)}, bf16[1,128,1024]{2,1,0:T(8,128)(2,1)}, bf16[2,144,2048]{2,1,0:T(8,128)(2,1)}) custom-call(s32[16]{0:T(128)} %layer_ref.1, bf16[2,144,2048]{2,1,0:T(8,128)(2,1)} %acts_hbm.1, bf16[2,144,2048]{2,1,0:T(8,128)(2,1)} %cot_hbm.1, bf16[1,1024,128]{2,1,0:T(8,128)(2,1)} %wg.1, ...), custom_call_target="tpu_custom_call" | custom-call | tf_op jit(solution)/shard_map/pallas_call | solution.py:200
  69.6 2.6 %shard_map.94 = (bf16[1,1024,128]{2,1,0:T(8,128)(2,1)}, bf16[1,1024,128]{2,1,0:T(8,128)(2,1)}, bf16[1,128,1024]{2,1,0:T(8,128)(2,1)}, bf16[2,144,2048]{2,1,0:T(8,128)(2,1)}) custom-call(bf16[1,1024,128]{2,1,0:T(8,128)(2,1)} %get-tuple-element.8.refs_0_, bf16[1,1024,128]{2,1,0:T(8,128)(2,1)} %get-tuple-element.9.refs_1_, ...), custom_call_target="tpu_custom_call" | custom-call | tf_op jit(solution)/shard_map/pallas_call | solution.py:241
